TPU v7x, 32 devices: a whole 2x2x4 slice. The times are simulated.
32 devices in a mesh: inline: 8 (over z, x), xline: 4 (over y, core).
Axes of the slice: x: 2, y: 2, z: 4, core: 2. Of those that a mesh axis runs over, the one named last changes fastest.
Arguments:
- traces: bfloat16 [8192, 2048], P(('inline', 'xline')), may hold values from -6 to 6
- trace_dest: int32 [8192, 1], P(('inline', 'xline')), may hold values from 0 to 31; in each aligned block of 256 rows (0 to 255, 256 to 511, ...) at most 16 rows name the same one
- trace_bin: int32 [8192], P(('inline', 'xline')), may hold values from 0 to 3
- trace_class: int32 [8192], P(('inline', 'xline')), may hold values from 0 to 7
- band_weights: bfloat16 [8, 16, 2, 128, 128], replicated, may hold values from -0.375 to 0.375
- conv_first: bfloat16 [32, 8, 3, 3, 3], replicated, may hold values from -0.4375 to 0.4375
- conv_second: bfloat16 [32, 32, 3, 3, 3], replicated, may hold values from -0.21875 to 0.21875
Outputs:
- regular: bfloat16 [32, 16, 8, 2048], P(None, 'inline', 'xline')
Inputs may be any that keep to these rules, and one draw needn't show every extreme that they name: `trace_dest`: among the 256 traces of one device no tile is named more than 16 times, a bound that some block reaches.
All inputs are finite; a program needn't handle non-finite values.
Results may differ from a plain program's by a relative error of at most 0.0065.
Values may be sent and summed in bfloat16 or wider, within the bound.
A program may use at most 256 MiB of HBM per device.

v0:
```python
import functools

import jax
import jax.numpy as jnp
from jax import lax
from jax.experimental import pallas as pl
from jax.experimental.pallas import tpu as pltpu
from jax.sharding import PartitionSpec as P

CLASSES = 8
BI = 2
BX = 2
GI = 2
LANES = 128
MESH = pl.DeviceIdType.MESH
F32 = jnp.float32
BF16 = jnp.bfloat16


def gelu(x):
    return 0.5 * x * (1.0 + jnp.tanh(0.7978845608028654 * (x + 0.044715 * (x * x * x))))


def split(value, size):
    if size & (size - 1):
        return lax.div(value, size), lax.rem(value, size)
    return value >> (size.bit_length() - 1), value & (size - 1)


def band_matrices(ch, XL, k1, k2, t1, t2):
    HR = ch * XL

    def banded(pieces, lane_x, x):
        low, mid, high = pieces
        zero = jnp.zeros_like(mid)
        return jnp.where(
            lane_x == x - 1, low, jnp.where(lane_x == x, mid, jnp.where(lane_x == x + 1, high, zero))
        )

    taps = [(di, dt) for di in range(3) for dt in range(3)]
    q1 = 9 * CLASSES
    lanes = lax.broadcasted_iota(jnp.int32, (q1, q1 * XL), 1)
    spread = jnp.where(
        split(lanes, XL)[0] == lax.broadcasted_iota(jnp.int32, (q1, q1 * XL), 0), 1.0, 0.0
    ).astype(BF16)
    pieces = []
    for dx in range(3):
        rows = jnp.concatenate([k1[di * 9 + dx * 3 + dt].astype(F32) for di, dt in taps], axis=0)
        pieces.append(
            lax.dot_general(
                rows.astype(BF16), spread, (((0,), (0,)), ((), ())), preferred_element_type=F32
            )
        )
    lane_x = split(lax.broadcasted_iota(jnp.int32, (ch, q1 * XL), 1), XL)[1]
    for x in range(XL):
        t1[x * ch:(x + 1) * ch, :] = banded(pieces, lane_x, x).astype(BF16)

    lane_x, lane_c = split(lax.broadcasted_iota(jnp.int32, (ch, HR), 1), ch)
    spread = jnp.where(lane_c == lax.broadcasted_iota(jnp.int32, (ch, HR), 0), 1.0, 0.0).astype(BF16)

    def tap(q, carry):
        first = (q // 3) * 9 + q % 3
        pieces = [jnp.dot(k2[first + dx * 3], spread, preferred_element_type=F32) for dx in range(3)]
        spot = pl.ds(pl.multiple_of(q * HR, LANES), HR)
        for x in range(XL):
            t2[x * ch:(x + 1) * ch, spot] = banded(pieces, lane_x, x).astype(BF16)
        return carry

    lax.fori_loop(0, 9, tap, 0)


def kernel(
    planes, xsize, rows, samples, ch,
    traces, target_h, bins_h, classes_h, band, k1_h, k2_h, out,
    target, bins, classes, k1, k2, codes, rx, crx, oh, own, counts, txz, rz, rl, ctx, crz, avg, anx, wts, vol, nxt, prv, v3, h3, t1, t2, outb,
    i_sem, w_sem, l_sem, o_sem, a_send, a_recv, c_send, c_recv, z_send, z_recv, l_recv, n_send, n_recv,
    e_send, e_recv, g_send, g_recv, y_send, y_recv,
):
    T = GI * xsize
    R = planes
    S = samples // T
    NCH = S // LANES
    I = GI * BI
    XL = xsize * BX
    CELLS = CLASSES * I * XL
    VR = CLASSES * XL
    HR = ch * XL
    inline = lax.axis_index("inline")
    xline = lax.axis_index("xline")
    z = lax.div(inline, GI)
    t = lax.rem(inline, GI) * xsize + xline

    def dev(zz, tt):
        return (zz * GI + lax.div(tt, xsize), lax.rem(tt, xsize))

    def mate(d):
        return lax.rem(t + d + T, T)

    def plane(d):
        return lax.rem(z + d + R, R)

    def remote(src, dst, ssem, rsem, target):
        return pltpu.make_async_remote_copy(
            src_ref=src, dst_ref=dst, send_sem=ssem, recv_sem=rsem,
            device_id=target, device_id_type=MESH,
        )

    weights = pltpu.make_async_copy(band.at[:, pl.ds(t * NCH, NCH)], wts, w_sem)
    local = []
    for c in range(NCH):
        col = pl.multiple_of(t * S + c * LANES, LANES)
        local.append(pltpu.make_async_copy(traces.at[:, pl.ds(col, LANES)], rx.at[c, 0], l_sem.at[c]))
    pairs = ((target_h, target), (bins_h, bins), (classes_h, classes), (k1_h, k1), (k2_h, k2))
    fetch = [pltpu.make_async_copy(a, b, i_sem.at[n]) for n, (a, b) in enumerate(pairs)]
    for copy in fetch:
        copy.start()

    barrier = pltpu.get_barrier_semaphore()
    partners = [dev(z, mate(d)) for d in range(1, T)]
    partners += [dev(plane(d), t) for d in range(1, R)]
    partners += [dev(plane(dz), mate(dt)) for dz in (-1, 1) for dt in (-1, 1)]
    for p in partners:
        pl.semaphore_signal(barrier, inc=1, device_id=p, device_id_type=MESH)

    for copy in fetch[:3]:
        copy.wait()
    dest_i, dest_x = split(target[...], xsize)
    dest_z, dest_a = split(dest_i, GI)
    bin_i, bin_x = split(bins[...], BX)
    code = dest_z * CELLS + (classes[...] * I + dest_a * BI + bin_i) * XL + dest_x * BX + bin_x
    codes[...] = jnp.broadcast_to(code, (8, rows))
    pl.semaphore_wait(barrier, len(partners))

    send_c, send_a = {}, {}
    for d in range(1, T):
        send_c[d] = remote(codes, crx.at[d], c_send.at[d], c_recv.at[d], dev(z, mate(d)))
        send_c[d].start()
    for c in range(NCH):
        for d in range(1, T):
            col = pl.multiple_of(mate(d) * S + c * LANES, LANES)
            send_a[c, d] = remote(
                traces.at[:, pl.ds(col, LANES)], rx.at[c, d],
                a_send.at[c * T + d], a_recv.at[c * T + d], dev(z, mate(d)),
            )
            send_a[c, d].start()
        local[c].start()
    weights.start()

    @pl.when(z == 0)
    def _():
        for ref in (vol, nxt, prv):
            ref[0:2] = jnp.zeros((2,) + ref.shape[1:], BF16)

    @pl.when(z == R - 1)
    def _():
        for ref in (vol, nxt, prv):
            ref[I + 2:I + 4] = jnp.zeros((2,) + ref.shape[1:], BF16)

    @pl.when(t == 0)
    def _():
        prv[...] = jnp.zeros(prv.shape, BF16)

    @pl.when(t == T - 1)
    def _():
        nxt[...] = jnp.zeros(nxt.shape, BF16)
        anx[...] = jnp.zeros(anx.shape, BF16)

    cell = lax.broadcasted_iota(jnp.int32, (CELLS, rows), 0)

    def one_hot(d, row):
        spot = pl.ds(pl.multiple_of(d * rows, LANES), rows)
        for r in range(R):
            oh[r, :, spot] = jnp.where(cell == row - r * CELLS, 1.0, 0.0).astype(BF16)

    def arrived_code(d, carry):
        remote(codes, crx.at[d], c_send.at[d], c_recv.at[d], dev(z, t)).wait_recv()
        one_hot(d, crx[d][0:1, :])
        return carry

    one_hot(0, codes[0:1, :])
    lax.fori_loop(1, T, arrived_code, 0)
    for copy in fetch[3:]:
        copy.wait()
    band_matrices(ch, XL, k1, k2, t1, t2)

    send_z, send_n = {}, {}
    outer = (z == 0) | (z == R - 1)

    def mirror(p):
        return jnp.where(z < 2, p, 3 - p)

    def hop(c, p, dst, rsem, r):
        return remote(txz.at[c, p], dst, z_send.at[c * R + p], rsem, dev(r, t))

    def hops(c):
        return {
            (0, True): hop(c, 0, rl.at[c], l_recv.at[c], mirror(1)),
            (0, False): hop(c, 0, rz.at[c, 0], z_recv.at[c * R], mirror(2)),
            (1, True): hop(c, 1, rz.at[c, 1], z_recv.at[c * R + 1], mirror(2)),
            (1, False): hop(c, 1, rz.at[c, 1], z_recv.at[c * R + 1], mirror(0)),
            (2, True): hop(c, 2, rz.at[c, 2], z_recv.at[c * R + 2], mirror(1)),
            (3, False): hop(c, 3, rz.at[c, 3], z_recv.at[c * R + 3], mirror(3)),
        }

    for c in range(NCH):
        local[c].wait()
        for d in range(1, T):
            send_a[c, d].wait_recv()
        data = rx[c].reshape(T * rows, LANES)
        data = jnp.concatenate([data, jnp.ones((T * rows, LANES), BF16)], axis=1)

        def summed(r):
            total = jnp.dot(oh[r], data, preferred_element_type=F32)
            if c == 0:
                counts[r] = total[:, LANES:]
            return total[:, :LANES]

        if R == 4:
            ways = hops(c)
            inner = jnp.logical_not(outer)

            def part(p, carry):
                r = mirror(jnp.where(outer, 3 - p, jnp.where(p == 0, 2, jnp.where(p == 3, 3, p - 1))))
                total = summed(r)
                txz[c, p] = total.astype(BF16)

                @pl.when((outer & (p == 3)) | (inner & (p == 2)))
                def _():
                    own[c] = total

                @pl.when(outer & (p == 0))
                def _():
                    ways[0, True].start()

                @pl.when(inner & (p == 0))
                def _():
                    ways[0, False].start()

                @pl.when(outer & (p == 1))
                def _():
                    ways[1, True].start()

                @pl.when(inner & (p == 1))
                def _():
                    ways[1, False].start()

                @pl.when(outer & (p == 2))
                def _():
                    ways[2, True].start()

                @pl.when(inner & (p == 3))
                def _():
                    ways[0, True].wait_recv()
                    txz[c, p] = (total + rl[c].astype(F32)).astype(BF16)
                    ways[3, False].start()

                return carry

            lax.fori_loop(0, 4, part, 0)
        else:
            for d in list(range(1, R)) + [0]:
                total = summed(plane(d))
                if d == 0:
                    own[c] = total
                else:
                    txz[c, d] = total.astype(BF16)
                    send_z[c, d] = hop(c, d, rz.at[c, d], z_recv.at[c * R + d], plane(d))
                    send_z[c, d].start()
        if c == 0:
            for d in range(1, R):
                ctx[d] = jnp.transpose(counts[plane(d)])[0:8]
                send_n[d] = remote(ctx.at[d], crz.at[d], n_send.at[d], n_recv.at[d], dev(plane(d), t))
                send_n[d].start()

    count = jnp.zeros((8, CELLS), F32)
    for d in range(1, R):
        send_n[d].wait_recv()
        count = count + crz[d]
    fold = counts[z] + jnp.transpose(jnp.broadcast_to(count[0:1], (LANES, CELLS)))
    fold = jnp.maximum(fold, 1.0)
    to_before = remote(avg.at[0], anx, e_send, e_recv, dev(z, mate(-1)))
    for c in range(NCH):
        if R == 4:
            ways = hops(c)

            @pl.when(outer)
            def _():
                ways[1, False].wait_recv()
                ways[3, False].wait_recv()
                own[c] = own[c] + rz[c, 1].astype(F32) + rz[c, 3].astype(F32)

            @pl.when(jnp.logical_not(outer))
            def _():
                for p in range(3):
                    ways[p, p == 2].wait_recv()
                own[c] = own[c] + rz[c, 0].astype(F32) + rz[c, 1].astype(F32) + rz[c, 2].astype(F32)

            total = own[c]
        else:
            total = own[c]
            for d in range(1, R):
                send_z[c, d].wait_recv()
                total = total + rz[c, d].astype(F32)
        avg[c] = (total / fold).astype(BF16)
        if c == 0:
            @pl.when(t > 0)
            def _():
                to_before.start()

    weights.wait()
    for k in range(NCH - 1):
        moveout(avg[k], avg[k + 1], wts, vol, k, I, XL)

    @pl.when(t < T - 1)
    def _():
        to_before.wait_recv()

    moveout(avg[NCH - 1], anx[...], wts, vol, NCH - 1, I, XL)

    def border(dz, dt):
        here, there = {0: ((2, I), (2, I)), 1: ((I, 2), (0, 2)), -1: ((2, 2), (I + 2, 2))}[dz]
        src = vol.at[pl.ds(*here)]
        if dt == 0:
            dst = vol.at[pl.ds(*there)]
        elif dt == -1:
            src = src.at[:, :, pl.ds(0, LANES)]
            dst = nxt.at[pl.ds(*there)]
        else:
            src = src.at[:, :, pl.ds(S - LANES, LANES)]
            dst = prv.at[pl.ds(*there)]
        index = (dz + 1) * 3 + dt + 1
        return remote(src, dst, g_send.at[index], g_recv.at[index], dev(plane(dz), mate(dt)))

    def inside(dz, dt):
        return (z + dz >= 0) & (z + dz < R) & (t + dt >= 0) & (t + dt < T)

    sides = [(0, -1), (0, 1), (-1, 0), (1, 0), (-1, -1), (-1, 1), (1, -1), (1, 1)]
    for dz, dt in sides:
        @pl.when(inside(dz, dt))
        def _(dz=dz, dt=dt):
            border(dz, dt).start()

    def arrive(pairs):
        for dz, dt in pairs:
            @pl.when(inside(-dz, -dt))
            def _(dz=dz, dt=dt):
                border(dz, dt).wait_recv()

    width = S + LANES
    half = lax.broadcasted_iota(jnp.int32, (VR, LANES), 1) < LANES // 2
    lane = lax.broadcasted_iota(jnp.int32, (HR, width), 1)
    keep = (lane < S) | ((lane < S + LANES // 2) & (t < T - 1)) | ((lane >= S + LANES // 2) & (t > 0))

    def spread(r):
        edge = jnp.where(half, nxt[r].astype(F32), prv[r].astype(F32))
        full = jnp.concatenate([vol[r].astype(F32), edge], axis=1)
        v3[r, 0:VR] = pltpu.roll(full, 1, 1).astype(BF16)
        v3[r, VR:2 * VR] = full.astype(BF16)
        v3[r, 2 * VR:3 * VR] = pltpu.roll(full, width - 1, 1).astype(BF16)

    def first(r):
        total = jnp.dot(t1[...], v3[pl.ds(r, 3)].reshape(9 * VR, width), preferred_element_type=F32)
        real = ((r > 0) | (z > 0)) & ((r < I + 1) | (z < R - 1))
        value = jnp.where(keep & real, gelu(total), 0.0)
        h3[r, 0:HR] = pltpu.roll(value, 1, 1)[:, :S].astype(BF16)
        h3[r, HR:2 * HR] = value[:, :S].astype(BF16)
        h3[r, 2 * HR:3 * HR] = pltpu.roll(value, width - 1, 1)[:, :S].astype(BF16)

    arrive(sides[:2])
    for r in range(2, I + 2):
        spread(r)
    for r in range(2, I):
        first(r)
    arrive(sides[2:])
    for r in (0, 1, I + 2, I + 3):
        spread(r)

    mine = lax.div(t, xsize)

    def tile_row(phase, n):
        a = 1 - mine if phase == 0 else mine
        return a, a * BI + (1 - a) * (1 - n) + a * n

    def shared(phase, n, k):
        a, r = tile_row(phase, n)
        b = lax.rem(xline + k, xsize)
        source = outb.at[r, pl.ds(b * BX, BX)]
        spot = out.at[r - a * BI, :, :, pl.ds(pl.multiple_of(t * S, LANES), S)]
        index = (phase * BI + n) * xsize + k
        if phase == 1 and k == 0:
            return pltpu.make_async_copy(source, spot, o_sem.at[n])
        return remote(source, spot, y_send.at[index], y_recv.at[index], dev(z, a * xsize + b))

    def landed(phase, n, k):
        a = 1 - mine if phase == 0 else mine
        r = (1 - mine) * (1 - n) + mine * n
        b = lax.rem(xline - k + xsize, xsize)
        spot = out.at[r, :, :, pl.ds(pl.multiple_of((a * xsize + b) * S, LANES), S)]
        index = (phase * BI + n) * xsize + k
        source = outb.at[r, pl.ds(b * BX, BX)]
        return remote(source, spot, y_send.at[index], y_recv.at[index], dev(z, a * xsize + b))

    steps = [(phase, n) for phase in range(2) for n in range(BI)]
    for phase, n in steps:
        a, r = tile_row(phase, n)
        first(r + a * 2)
        total = jnp.dot(t2[...], h3[pl.ds(r, 3)].reshape(9 * HR, S), preferred_element_type=F32)
        outb[r] = total.astype(BF16).reshape(XL, ch, S)
        for k in range(xsize):
            shared(phase, n, k).start()
    for phase, n in steps:
        for k in range(xsize):
            if (phase, k) == (1, 0):
                shared(phase, n, k).wait()
            else:
                landed(phase, n, k).wait_recv()
                shared(phase, n, k).wait_send()

    for copy in (send_c, send_a, send_z, send_n):
        for item in copy.values():
            item.wait_send()
    if R == 4:
        for c in range(NCH):
            ways = hops(c)
            for p in range(2):
                ways[p, False].wait_send()

            @pl.when(outer)
            def _():
                ways[2, True].wait_send()

            @pl.when(jnp.logical_not(outer))
            def _():
                ways[3, False].wait_send()

    @pl.when(t > 0)
    def _():
        to_before.wait_send()

    for dz, dt in sides:
        @pl.when(inside(dz, dt))
        def _(dz=dz, dt=dt):
            border(dz, dt).wait_send()


def moveout(block, following, wts, vol, k, I, XL):
    bins = I * XL
    moved = []
    for c in range(CLASSES):
        both = jnp.concatenate(
            [block[c * bins:(c + 1) * bins], following[c * bins:(c + 1) * bins]], axis=1
        )
        moved.append(jnp.dot(both, wts[c, k], preferred_element_type=F32))
    for i in range(I):
        rows = jnp.concatenate([m[i * XL:(i + 1) * XL] for m in moved], axis=0)
        vol[2 + i, :, k * LANES:(k + 1) * LANES] = rows.astype(BF16)


def per_device(traces, trace_dest, trace_bin, trace_class, band_weights, conv_first, conv_second):
    inline_size = lax.axis_size("inline")
    xsize = lax.axis_size("xline")
    planes = inline_size // GI
    rows, samples = traces.shape
    ch = conv_first.shape[0]
    T = GI * xsize
    R = planes
    S = samples // T
    NCH = S // LANES
    I = GI * BI
    XL = xsize * BX
    CELLS = CLASSES * I * XL
    VR = CLASSES * XL
    HR = ch * XL
    nb, bw = band_weights.shape[1], band_weights.shape[-1]

    band = band_weights.reshape(CLASSES, nb, 2 * bw, bw)
    k1 = jnp.transpose(conv_first, (2, 3, 4, 1, 0)).reshape(27, CLASSES, ch)
    k2 = jnp.transpose(conv_second, (2, 3, 4, 0, 1)).reshape(27, ch, ch)

    vmem = pl.BlockSpec(memory_space=pltpu.VMEM)
    hbm = pl.BlockSpec(memory_space=pltpu.HBM)
    dma = pltpu.SemaphoreType.DMA
    out = pl.pallas_call(
        functools.partial(kernel, planes, xsize, rows, samples, ch),
        out_shape=jax.ShapeDtypeStruct((BI, BX, ch, samples), BF16),
        in_specs=[hbm] * 7,
        out_specs=vmem,
        scratch_shapes=[
            pltpu.VMEM((1, rows), jnp.int32),
            pltpu.VMEM((1, rows), jnp.int32),
            pltpu.VMEM((1, rows), jnp.int32),
            pltpu.VMEM((27, CLASSES, ch), BF16),
            pltpu.VMEM((27, ch, ch), BF16),
            pltpu.VMEM((8, rows), jnp.int32),
            pltpu.VMEM((NCH, T, rows, LANES), BF16),
            pltpu.VMEM((T, 8, rows), jnp.int32),
            pltpu.VMEM((R, CELLS, T * rows), BF16),
            pltpu.VMEM((NCH, CELLS, LANES), F32),
            pltpu.VMEM((R, CELLS, LANES), F32),
            pltpu.VMEM((NCH, R, CELLS, LANES), BF16),
            pltpu.VMEM((NCH, R, CELLS, LANES), BF16),
            pltpu.VMEM((NCH, CELLS, LANES), BF16),
            pltpu.VMEM((R, 8, CELLS), F32),
            pltpu.VMEM((R, 8, CELLS), F32),
            pltpu.VMEM((NCH, CELLS, LANES), BF16),
            pltpu.VMEM((CELLS, LANES), BF16),
            pltpu.VMEM((CLASSES, NCH, 2 * bw, bw), BF16),
            pltpu.VMEM((I + 4, VR, S), BF16),
            pltpu.VMEM((I + 4, VR, LANES), BF16),
            pltpu.VMEM((I + 4, VR, LANES), BF16),
            pltpu.VMEM((I + 4, 3 * VR, S + LANES), BF16),
            pltpu.VMEM((I + 2, 3 * HR, S), BF16),
            pltpu.VMEM((HR, 9 * VR), BF16),
            pltpu.VMEM((HR, 9 * HR), BF16),
            pltpu.VMEM((I, XL, ch, S), BF16),
            dma((5,)), dma, dma((NCH,)), dma((BI,)),
            dma((NCH * T,)), dma((NCH * T,)),
            dma((T,)), dma((T,)),
            dma((NCH * R,)), dma((NCH * R,)), dma((NCH,)),
            dma((R,)), dma((R,)),
            dma, dma,
            dma((9,)), dma((9,)),
            dma((BI * T,)), dma((BI * T,)),
        ],
        compiler_params=pltpu.CompilerParams(
            collective_id=0, has_side_effects=True, vmem_limit_bytes=(61440 if T <= 8 else 60 * 1024) * 1024
        ),
        name="regularize",
    )(
        traces, trace_dest.reshape(1, rows), trace_bin.reshape(1, rows), trace_class.reshape(1, rows),
        band, k1, k2,
    )
    return jnp.transpose(out, (2, 0, 1, 3))


def solution(mesh):
    return jax.shard_map(
        per_device,
        mesh=mesh,
        in_specs=(
            P(("inline", "xline"), None),
            P(("inline", "xline"), None),
            P(("inline", "xline")),
            P(("inline", "xline")),
            P(),
            P(),
            P(),
        ),
        out_specs=P(None, "inline", "xline", None),
        check_vma=False,
    )
```

profile of v0, /device:TPU:0, one launch (start us, length us, event | category | flops | bytes accessed | tf_op | source)
XLA Modules:
  0.0 46.4 jit_solution(13261699698614570772)
XLA Ops:
  0.0 44.0 %regularize.1 = bf16[2,2,32,2048]{3,2,1,0:T(8,128)(2,1)} custom-call(bf16[256,2048]{1,0:T(8,128)(2,1)} %traces.1, s32[1,256]{1,0:T(1,128)} %bitcast.15, s32[1,256]{1,0:T(1,128)} %bitcast.16, s32[1,256]{1,0:T(1,128)} %bitcast.17, bf16[8,16,256,128]{3,2,1,0:T(8,128)(2,1)} %bitcast.11, bf16[27,8,32]{2,1,0:T(8,128)(2,1)} %bitcast.14, bf16[27,32,32]{2,1,0:T(8,128)(2,1)} %bitcast.13), custom_call_target="tpu_custom_call" | custom-call | tf_op jit(solution)/shard_map/regularize/pallas_call | solution.py:483
  44.0 2.4 %copy.8 = bf16[32,2,2,2048]{3,2,1,0:T(2,128)(2,1)} copy(bf16[32,2,2,2048]{3,0,2,1:T(8,128)(2,1)} %bitcast.12) | data formatting | bytes 1048576 | tf_op jit(solution)/shard_map/transpose | solution.py:533
where the time goes:
time: 46.5 us; the launch traced here: 46.4 us
  Pallas kernels  44 us (95%)
  local copies, waits for them, and re-layouts  2.38 us (5%)
    pallas_call x1, Pallas kernels, per_device(): pl.pallas_call(functools.partial(kernel, planes, xsize, rows, samples, ch...  44 us
    transpose x1, local copies, waits for them, and re-layouts, per_device(): return jnp.transpose(out, (2, 0, 1, 3))  2.38 us

commit v1 on v0

--- a/solution.py
+++ b/solution.py
@@ -72,7 +72,7 @@
 def kernel(
     planes, xsize, rows, samples, ch,
     traces, target_h, bins_h, classes_h, band, k1_h, k2_h, out,
-    target, bins, classes, k1, k2, codes, rx, crx, oh, own, counts, txz, rz, rl, ctx, crz, avg, anx, wts, vol, nxt, prv, v3, h3, t1, t2, outb,
+    target, bins, classes, k1, k2, codes, rx, crx, oh, own, counts, txz, rz, rl, ctx, crz, avg, anx, wts, vol, nxt, prv, low, high, v3, h3, t1, t2, outb,
     i_sem, w_sem, l_sem, o_sem, a_send, a_recv, c_send, c_recv, z_send, z_recv, l_recv, n_send, n_recv,
     e_send, e_recv, g_send, g_recv, y_send, y_recv,
 ):
@@ -148,13 +148,15 @@
 
     @pl.when(z == 0)
     def _():
-        for ref in (vol, nxt, prv):
-            ref[0:2] = jnp.zeros((2,) + ref.shape[1:], BF16)
+        vol[0:2] = jnp.zeros((2,) + vol.shape[1:], BF16)
+        nxt[0] = jnp.zeros(nxt.shape[1:], BF16)
+        prv[0] = jnp.zeros(prv.shape[1:], BF16)
 
     @pl.when(z == R - 1)
     def _():
-        for ref in (vol, nxt, prv):
-            ref[I + 2:I + 4] = jnp.zeros((2,) + ref.shape[1:], BF16)
+        vol[I + 2:I + 4] = jnp.zeros((2,) + vol.shape[1:], BF16)
+        nxt[2] = jnp.zeros(nxt.shape[1:], BF16)
+        prv[2] = jnp.zeros(prv.shape[1:], BF16)
 
     @pl.when(t == 0)
     def _():
@@ -317,17 +319,30 @@
 
     moveout(avg[NCH - 1], anx[...], wts, vol, NCH - 1, I, XL)
 
+    pair = lax.broadcasted_iota(jnp.int32, (VR, LANES), 1) >> 1
+
+    def turned(x, by):
+        return pltpu.roll(x, by % LANES, 1) if by % LANES else x
+
+    first_two = jnp.zeros((VR, LANES), F32)
+    last_two = jnp.zeros((VR, LANES), F32)
+    for i in range(I):
+        begin = turned(vol[2 + i, :, 0:LANES].astype(F32), 2 * i)
+        end = turned(vol[2 + i, :, S - LANES:S].astype(F32), -2 * i)
+        first_two = jnp.where(pair == i, begin, first_two)
+        last_two = jnp.where(pair == LANES // 2 - 1 - i, end, last_two)
+    low[...] = first_two.astype(BF16)
+    high[...] = last_two.astype(BF16)
+
     def border(dz, dt):
         here, there = {0: ((2, I), (2, I)), 1: ((I, 2), (0, 2)), -1: ((2, 2), (I + 2, 2))}[dz]
         src = vol.at[pl.ds(*here)]
         if dt == 0:
             dst = vol.at[pl.ds(*there)]
         elif dt == -1:
-            src = src.at[:, :, pl.ds(0, LANES)]
-            dst = nxt.at[pl.ds(*there)]
+            src, dst = low.at[...], nxt.at[1 - dz]
         else:
-            src = src.at[:, :, pl.ds(S - LANES, LANES)]
-            dst = prv.at[pl.ds(*there)]
+            src, dst = high.at[...], prv.at[1 - dz]
         index = (dz + 1) * 3 + dt + 1
         return remote(src, dst, g_send.at[index], g_recv.at[index], dev(plane(dz), mate(dt)))
 
@@ -352,7 +367,10 @@
     keep = (lane < S) | ((lane < S + LANES // 2) & (t < T - 1)) | ((lane >= S + LANES // 2) & (t > 0))
 
     def spread(r):
-        edge = jnp.where(half, nxt[r].astype(F32), prv[r].astype(F32))
+        source, i = (0, I - 2 + r) if r < 2 else (1, r - 2) if r < I + 2 else (2, r - I - 2)
+        edge = jnp.where(
+            half, turned(nxt[source].astype(F32), -2 * i), turned(prv[source].astype(F32), 2 * i)
+        )
         full = jnp.concatenate([vol[r].astype(F32), edge], axis=1)
         v3[r, 0:VR] = pltpu.roll(full, 1, 1).astype(BF16)
         v3[r, VR:2 * VR] = full.astype(BF16)
@@ -477,14 +495,13 @@
     k1 = jnp.transpose(conv_first, (2, 3, 4, 1, 0)).reshape(27, CLASSES, ch)
     k2 = jnp.transpose(conv_second, (2, 3, 4, 0, 1)).reshape(27, ch, ch)
 
-    vmem = pl.BlockSpec(memory_space=pltpu.VMEM)
     hbm = pl.BlockSpec(memory_space=pltpu.HBM)
     dma = pltpu.SemaphoreType.DMA
     out = pl.pallas_call(
         functools.partial(kernel, planes, xsize, rows, samples, ch),
         out_shape=jax.ShapeDtypeStruct((BI, BX, ch, samples), BF16),
         in_specs=[hbm] * 7,
-        out_specs=vmem,
+        out_specs=hbm,
         scratch_shapes=[
             pltpu.VMEM((1, rows), jnp.int32),
             pltpu.VMEM((1, rows), jnp.int32),
@@ -506,8 +523,10 @@
             pltpu.VMEM((CELLS, LANES), BF16),
             pltpu.VMEM((CLASSES, NCH, 2 * bw, bw), BF16),
             pltpu.VMEM((I + 4, VR, S), BF16),
-            pltpu.VMEM((I + 4, VR, LANES), BF16),
-            pltpu.VMEM((I + 4, VR, LANES), BF16),
+            pltpu.VMEM((3, VR, LANES), BF16),
+            pltpu.VMEM((3, VR, LANES), BF16),
+            pltpu.VMEM((VR, LANES), BF16),
+            pltpu.VMEM((VR, LANES), BF16),
             pltpu.VMEM((I + 4, 3 * VR, S + LANES), BF16),
             pltpu.VMEM((I + 2, 3 * HR, S), BF16),
             pltpu.VMEM((HR, 9 * VR), BF16),

time: 46.5 us -> 45.5 us (0.978)
  Pallas kernels: 44 us -> 42.9 us
    pallas_call x1, Pallas kernels: 44 us -> 42.9 us  [per_device(): pl.pallas_call(functools.partial(kernel, planes, xsize, rows, samples, ch...]
where the time goes in v1:
time: 45.5 us; the launch traced here: 45.3 us
  Pallas kernels  42.9 us (94%)
  local copies, waits for them, and re-layouts  2.38 us (5%)
    pallas_call x1, Pallas kernels, per_device(): pl.pallas_call(functools.partial(kernel, planes, xsize, rows, samples, ch...  42.9 us
    transpose x1, local copies, waits for them, and re-layouts, per_device(): return jnp.transpose(out, (2, 0, 1, 3))  2.38 us

profile of v1, /device:TPU:0, one launch (start us, length us, event | category | flops | bytes accessed | tf_op | source)
XLA Modules:
  0.0 45.3 jit_solution(14939508671572046547)
XLA Ops:
  0.0 42.9 %regularize.1 = bf16[2,2,32,2048]{3,2,1,0:T(8,128)(2,1)} custom-call(bf16[256,2048]{1,0:T(8,128)(2,1)} %traces.1, s32[1,256]{1,0:T(1,128)} %bitcast.15, s32[1,256]{1,0:T(1,128)} %bitcast.16, s32[1,256]{1,0:T(1,128)} %bitcast.17, bf16[8,16,256,128]{3,2,1,0:T(8,128)(2,1)} %bitcast.11, bf16[27,8,32]{2,1,0:T(8,128)(2,1)} %bitcast.14, bf16[27,32,32]{2,1,0:T(8,128)(2,1)} %bitcast.13), custom_call_target="tpu_custom_call" | custom-call | tf_op jit(solution)/shard_map/regularize/pallas_call | solution.py:500
  42.9 2.4 %copy.8 = bf16[32,2,2,2048]{3,2,1,0:T(2,128)(2,1)} copy(bf16[32,2,2,2048]{3,0,2,1:T(8,128)(2,1)} %bitcast.12) | data formatting | bytes 1048576 | tf_op jit(solution)/shard_map/transpose | solution.py:552

commit v2 on v1

--- a/solution.py
+++ b/solution.py
@@ -135,8 +135,10 @@
     for d in range(1, T):
         send_c[d] = remote(codes, crx.at[d], c_send.at[d], c_recv.at[d], dev(z, mate(d)))
         send_c[d].start()
-    for c in range(NCH):
-        for d in range(1, T):
+    far_first = sorted(range(1, T), key=lambda d: abs(d - T // 2))
+
+    def send_chunk(c):
+        for d in far_first:
             col = pl.multiple_of(mate(d) * S + c * LANES, LANES)
             send_a[c, d] = remote(
                 traces.at[:, pl.ds(col, LANES)], rx.at[c, d],
@@ -144,6 +146,8 @@
             )
             send_a[c, d].start()
         local[c].start()
+
+    send_chunk(0)
     weights.start()
 
     @pl.when(z == 0)
@@ -181,6 +185,8 @@
 
     one_hot(0, codes[0:1, :])
     lax.fori_loop(1, T, arrived_code, 0)
+    for c in range(1, NCH):
+        send_chunk(c)
     for copy in fetch[3:]:
         copy.wait()
     band_matrices(ch, XL, k1, k2, t1, t2)

time: 45.5 us -> 45.5 us (level)
  no operation moved by 1% of the time
where the time goes in v2:
time: 45.5 us; the launch traced here: 45.3 us
  Pallas kernels  43 us (95%)
  local copies, waits for them, and re-layouts  2.38 us (5%)
    pallas_call x1, Pallas kernels, per_device(): pl.pallas_call(functools.partial(kernel, planes, xsize, rows, samples, ch...  43 us
    transpose x1, local copies, waits for them, and re-layouts, per_device(): return jnp.transpose(out, (2, 0, 1, 3))  2.38 us

profile of v2, /device:TPU:0, one launch (start us, length us, event | category | flops | bytes accessed | tf_op | source)
XLA Modules:
  0.0 45.3 jit_solution(16383409156854297121)
XLA Ops:
  0.0 43.0 %regularize.1 = bf16[2,2,32,2048]{3,2,1,0:T(8,128)(2,1)} custom-call(bf16[256,2048]{1,0:T(8,128)(2,1)} %traces.1, s32[1,256]{1,0:T(1,128)} %bitcast.15, s32[1,256]{1,0:T(1,128)} %bitcast.16, s32[1,256]{1,0:T(1,128)} %bitcast.17, bf16[8,16,256,128]{3,2,1,0:T(8,128)(2,1)} %bitcast.11, bf16[27,8,32]{2,1,0:T(8,128)(2,1)} %bitcast.14, bf16[27,32,32]{2,1,0:T(8,128)(2,1)} %bitcast.13), custom_call_target="tpu_custom_call" | custom-call | tf_op jit(solution)/shard_map/regularize/pallas_call | solution.py:506
  43.0 2.4 %copy.8 = bf16[32,2,2,2048]{3,2,1,0:T(2,128)(2,1)} copy(bf16[32,2,2,2048]{3,0,2,1:T(8,128)(2,1)} %bitcast.12) | data formatting | bytes 1048576 | tf_op jit(solution)/shard_map/transpose | solution.py:558
